TPU v7x, 512 devices: a whole 4x4x16 slice. The times are simulated.
512 devices in a mesh: dp: 64 (over y, z_lo, core), hd: 8 (over z_hi, x).
Axes of the slice: x: 4, y: 4, z: 16 (z_hi: 2, z_lo: 8; z = z_hi * 8 + z_lo), core: 2. Of those that a mesh axis runs over, the one named last changes fastest.
Arguments:
- query: bfloat16 [256, 2, 64, 576], P('dp', None, 'hd')
- cache: bfloat16 [256, 192, 576], P('dp')
- lengths: int32 [256], P('dp'), may hold values from 2 to 192
- counts: int32 [64], P('dp'), may hold values from 1 to 4
- value_up: bfloat16 [64, 512, 128], P('hd'), may hold values from -0.25 to 0.25
- out_proj: bfloat16 [8192, 7168], P('hd', 'dp'), may hold values from -0.25 to 0.25
- residual: bfloat16 [512, 7168], P('dp', 'hd'), may hold values from -6 to 6
- norm_gain: float32 [7168], P('hd'), may hold values from 0.25 to 1.75
- gate_weight: bfloat16 [7168, 18432], P('hd', 'dp'), may hold values from -0.0625 to 0.0625
- up_weight: bfloat16 [7168, 18432], P('hd', 'dp'), may hold values from -0.0625 to 0.0625
- down_weight: bfloat16 [18432, 7168], P('dp', 'hd'), may hold values from -0.046875 to 0.046875
Outputs:
- layer_out: bfloat16 [512, 7168], P('dp', 'hd')
All inputs are finite; a program needn't handle non-finite values.
Results may differ from a plain program's by a relative error of at most 0.015.
Values may be sent and summed in bfloat16 or wider, within the bound.
A program may use at most 64 MiB of HBM per device.

v0:
```python
import jax
import jax.numpy as jnp
from jax import lax
from jax.sharding import PartitionSpec as P

D = 7168
ROPE = 64
VHEAD = 128


def per_device(
    query,
    cache,
    lengths,
    counts,
    value_up,
    out_proj,
    residual,
    norm_gain,
    gate_weight,
    up_weight,
    down_weight,
):
    slots = query.shape[0]
    qtok = query.shape[1]
    latent_width = value_up.shape[1]
    positions = cache.shape[1]
    scores = jnp.einsum("sthc,spc->sthp", query, cache, preferred_element_type=jnp.float32)
    scores = scores / jnp.sqrt(jnp.float32(VHEAD + ROPE))
    limit = lengths[:, None] - qtok + 1 + jnp.arange(qtok, dtype=jnp.int32)[None, :]
    keep = jnp.arange(positions, dtype=jnp.int32)[None, None, None, :] < limit[:, :, None, None]
    scores = jnp.where(keep, scores, -1e30)
    top = jnp.max(scores, axis=-1, keepdims=True)
    expo = jnp.exp(scores - top)
    weights = (expo / jnp.sum(expo, axis=-1, keepdims=True)).astype(jnp.bfloat16)
    latent = jnp.einsum(
        "sthp,spc->sthc", weights, cache[:, :, :latent_width], preferred_element_type=jnp.float32
    ).astype(jnp.bfloat16)
    livef = (jnp.arange(slots, dtype=jnp.int32) < counts[0]).astype(jnp.float32)
    heads = jnp.einsum("sthc,hcv->sthv", latent, value_up, preferred_element_type=jnp.float32)
    heads = (heads * livef[:, None, None, None]).astype(jnp.bfloat16)
    head_out = heads.reshape(slots * qtok, heads.shape[2] * heads.shape[3])
    partial_value = jnp.dot(
        lax.all_gather(head_out, "dp", axis=0, tiled=True),
        out_proj,
        preferred_element_type=jnp.float32,
    )
    moved = lax.all_to_all(partial_value, "dp", split_axis=0, concat_axis=1, tiled=True)
    attn = lax.psum_scatter(moved, "hd", scatter_dimension=1, tiled=True)
    attn = attn.astype(jnp.bfloat16)
    state = (residual.astype(jnp.float32) + attn.astype(jnp.float32)).astype(jnp.bfloat16)
    gathered = lax.all_gather(state, "dp", axis=0, tiled=True)
    wholef = gathered.astype(jnp.float32)
    sumsq = jnp.sum(wholef * wholef, axis=1)
    scaled = (wholef * norm_gain[None, :]).astype(jnp.bfloat16)
    gate_part = jnp.dot(scaled, gate_weight, preferred_element_type=jnp.float32)
    up_part = jnp.dot(scaled, up_weight, preferred_element_type=jnp.float32)
    gate_sum, up_sum, total_sq = lax.psum((gate_part, up_part, sumsq), "hd")
    inverse = lax.rsqrt(total_sq / D + 1e-06)[:, None]
    hidden = (jax.nn.silu(gate_sum * inverse) * (up_sum * inverse)).astype(jnp.bfloat16)
    down = lax.psum_scatter(
        jnp.dot(hidden, down_weight, preferred_element_type=jnp.float32),
        "dp",
        scatter_dimension=0,
        tiled=True,
    )
    token_live = jnp.repeat(livef, qtok)[:, None]
    return ((state.astype(jnp.float32) + down) * token_live).astype(jnp.bfloat16)


def solution(mesh):
    return jax.shard_map(
        per_device,
        mesh=mesh,
        in_specs=(
            P("dp", None, "hd", None),
            P("dp", None, None),
            P("dp"),
            P("dp"),
            P("hd", None, None),
            P("hd", "dp"),
            P("dp", "hd"),
            P("hd"),
            P("hd", "dp"),
            P("hd", "dp"),
            P("dp", "hd"),
        ),
        out_specs=P("dp", "hd"),
        check_vma=False,
    )
```

profile of v0, /device:TPU:1, one launch (start us, length us, event | category | flops | bytes accessed | tf_op | source)
XLA Modules:
  0.0 1391.5 jit_solution(5855858224323762385)
XLA Ops:
  6.5 0.8 broadcast_add_fusion
  7.3 0.1 iota_add_fusion
  7.4 0.1 iota_compare_fusion
  7.5 1.7 fusion.5
  9.1 0.2 fusion.24
  9.3 1.4 convolution_convert_fusion
  11.4 0.3 fusion.7
  11.7 0.6 copy.31
  12.3 0.0 all-gather.2.cloned.1.call-update
  12.3 0.0 reduce-scatter.2.cloned.1.call-start
  12.4 125.0 %all-gather.2.cloned.1.call-done = bf16[512,1024]{1,0:T(8,128)(2,1)} async-done(((bf16[8,1024]{1,0:T(8,128)(2,1)}), bf16[512,1024]{1,0:T(8,128)(2,1)}) %all-gather.2.cloned.1.call-update) | async-done | bytes 1048592 | tf_op jit(solution)/shard_map/all_gather | solution.py:44
  137.4 1.7 convolution_bitcast_fusion
  139.1 26.4 %all_to_all.19 = f32[64,8,112]{2,1,0:T(8,128)S(1)} all-to-all(f32[64,8,112]{2,1,0:T(8,128)S(1)} %convolution_bitcast_fusion), channel_id=1, replica_groups=mesh['dp'=64,'hd'=8] {'dp'}, dimensions={0} | all-to-all | bytes 458752 | tf_op jit(solution)/shard_map/all_to_all | solution.py:48
  165.5 0.1 copy.22
  165.6 0.9 all_to_all.17
  166.4 0.0 reduce-scatter.2.cloned.1.call-update
  166.5 0.0 all-reduce.7.cloned.1.call-start
  166.5 95.5 %reduce-scatter.2.cloned.1.call-done = f32[8,896]{1,0:T(8,128)} async-done(((f32[8,7168]{1,0:T(8,128)}), f32[8,896]{1,0:T(8,128)}) %reduce-scatter.2.cloned.1.call-update) | async-done | bytes 28688 | tf_op jit(solution)/shard_map/reduce_scatter | solution.py:49
  262.0 0.8 add_convert_fusion
  262.7 121.0 %all_gather.7 = bf16[512,896]{1,0:T(8,128)(2,1)S(1)} all-gather(bf16[8,896]{1,0:T(8,128)(2,1)S(1)} %add_convert_fusion), channel_id=1, replica_groups=mesh['dp'=64,'hd'=8] {'dp'}, dimensions={0}, use_global_device_ids=true | all-gather | bytes 931840 | tf_op jit(solution)/shard_map/all_gather | solution.py:52
  383.7 1.3 fusion.10
  385.1 1.3 fusion.12
  386.4 0.0 all-reduce.5.cloned.1.call-start
  386.5 0.3 fusion.2
  386.7 39.0 %psum.22 = f32[512]{0:T(512)S(1)} all-reduce(f32[512]{0:T(512)S(1)} %fusion.2), channel_id=1, replica_groups=mesh['dp'=64,'hd'=8] {'hd'}, use_global_device_ids=true, to_apply=%region_5.6 | all-reduce | flops 512 | bytes 4096 | tf_op jit(solution)/shard_map/psum | solution.py:58
  425.8 130.9 %all-reduce.7.cloned.1.call-done = (f32[512,288]{0,1:T(8,128)}, f32[512,288]{0,1:T(8,128)}) async-done(((f32[512,288]{0,1:T(8,128)}, f32[512,288]{0,1:T(8,128)}), (f32[512,288]{0,1:T(8,128)}, f32[512,288]{0,1:T(8,128)})) %all-reduce.7.cloned.1.call-update) | async-done | bytes 1179664 | tf_op jit(solution)/shard_map/psum | solution.py:58
  556.6 3.3 fusion.16
  559.9 0.1 broadcast_in_dim.16
  560.0 0.1 mul.61
  560.1 1.3 dynamic-slice
  562.0 821.6 %all-reduce.5.cloned.1.call-done = f32[512,896]{1,0:T(8,128)} async-done(((f32[512,896]{1,0:T(8,128)}), f32[512,896]{1,0:T(8,128)}) %all-reduce.5.cloned.1.call-update) | async-done | bytes 1835024
  1383.6 1.4 fusion.22
  (20 shorter events, 0.1 us)
Async XLA Ops:
  6.5 4.9 copy-start
  6.5 130.9 %copy-start.1 = (bf16[1024,112]{0,1:T(8,128)(2,1)S(1)}, bf16[1024,112]{0,1:T(8,128)(2,1)}, u32[]{:S(2)}) copy-start(bf16[1024,112]{0,1:T(8,128)(2,1)} %param.16) | copy-start | bytes 688132
  6.5 130.9 %all-gather.2.cloned.1.call-start = ((), (), s32[]{:S(2)}) async-start(), calls=%async_computation.2 | async-start | bytes 1064960 | tf_op jit(solution)/shard_map/all_gather | solution.py:44
  11.7 250.3 %copy-start.2 = (bf16[8,896]{1,0:T(8,128)(2,1)S(1)}, bf16[8,896]{1,0:T(8,128)(2,1)}, u32[]{:S(2)}) copy-start(bf16[8,896]{1,0:T(8,128)(2,1)} %param.17) | copy-start | bytes 43012
  12.3 371.4 %copy-start.3 = (bf16[896,288]{0,1:T(8,128)(2,1)S(1)}, bf16[896,288]{0,1:T(8,128)(2,1)}, u32[]{:S(2)}) copy-start(bf16[896,288]{0,1:T(8,128)(2,1)} %param.20) | copy-start | bytes 1548292
  12.3 371.4 %copy-start.6 = (f32[896]{0:T(1024)S(1)}, f32[896]{0:T(1024)}, u32[]{:S(2)}) copy-start(f32[896]{0:T(1024)} %param.18) | copy-start | bytes 10756
  12.3 249.6 %reduce-scatter.2.cloned.1.call-start = ((), (), s32[]{:S(2)}) async-start(), calls=%async_computation.3 | async-start | bytes 258048 | tf_op jit(solution)/shard_map/reduce_scatter | solution.py:49
  165.6 219.5 %copy-start.4 = (bf16[896,288]{0,1:T(8,128)(2,1)S(1)}, bf16[896,288]{0,1:T(8,128)(2,1)}, u32[]{:S(2)}) copy-start(bf16[896,288]{0,1:T(8,128)(2,1)} %param.19) | copy-start | bytes 1548292
  166.5 390.1 %all-reduce.7.cloned.1.call-start = ((), (), s32[]{:S(2)}) async-start(), calls=%async_computation.5 | async-start | bytes 2359296 | tf_op jit(solution)/shard_map/psum | solution.py:58
  385.1 171.6 %copy-start.5 = (bf16[288,896]{1,0:T(8,128)(2,1)S(1)}, bf16[288,896]{1,0:T(8,128)(2,1)}, u32[]{:S(2)}) copy-start(bf16[288,896]{1,0:T(8,128)(2,1)} %param.21) | copy-start | bytes 1548292
  386.4 997.2 %all-reduce.5.cloned.1.call-start = ((), (), s32[]{:S(2)}) async-start(), calls=%async_computation.4 | async-start | bytes 3670016
Sparse Core Ops, SparseCore 0:
  12.4 124.9 all-gather.1
  166.6 95.3 reduce-scatter.1
  386.5 170.0 all-reduce.6
  560.0 823.4 all-reduce.4
where the time goes:
time: 1390 us
  waiting for transfers between devices  1170 us (84%)
  blocking collectives  186 us (13%)
  between operations  14.5 us (1%)
    unnamed x5, waiting for transfers between devices  822 us
    psum x1, waiting for transfers between devices, per_device(): gate_sum, up_sum, total_sq = lax.psum((gate_part, up_part, sumsq), 'hd')  131 us
    all_gather x1, waiting for transfers between devices, per_device(): lax.all_gather(head_out, 'dp', axis=0, tiled=True)  125 us
    all_gather x1, blocking collectives, per_device(): gathered = lax.all_gather(state, 'dp', axis=0, tiled=True)  121 us
    reduce_scatter x1, waiting for transfers between devices, per_device(): attn = lax.psum_scatter(moved, 'hd', scatter_dimension=1, tiled=True)  95.5 us
    psum x1, blocking collectives, per_device(): gate_sum, up_sum, total_sq = lax.psum((gate_part, up_part, sumsq), 'hd')  39 us
  transfers between devices with their start and end apart: 4, of which 4 were waited for; matrix products, arithmetic and copies ran while one was open for 0% of the time, Pallas kernels for 0%

commit v1 on v0

v1 whole, which is shorter than its diff:
```python
import functools

import jax
import jax.numpy as jnp
from jax import lax
from jax.experimental import pallas as pl
from jax.experimental.pallas import tpu as pltpu
from jax.sharding import PartitionSpec as P

MESH = pl.DeviceIdType.MESH
F32, BF16 = jnp.float32, jnp.bfloat16
D = 7168
SLOTS, QTOK, HEADS, LAT, QK, POS = 4, 2, 8, 512, 576, 192
NX, NY, NZ, NSEM = 4, 4, 8, 256
OUTCOL, FEAT, UNITS = 112, 896, 288


def flip(value, mask, bits=3):
    out = 0
    for i in range(bits):
        bit = lax.rem(lax.div(value, 1 << i), 2)
        out = out + (1 - bit if (mask >> i) & 1 else bit) * (1 << i)
    return out


def kernel(
    query, cache, lengths, counts, value_up, out_proj, residual, norm_gain, gate_w, up_w, down_w,
    out,
    lat, hsc, tf, g1, w1, pb, rx, sb, rz, rsp, rt, gn, st, so, g2, w2, gb, rxg, sx, rzh, hb, w3,
    dsend, drecv, eb, fr, fb, zr, osum, orx, stf, ss, rs,
):
    dp, hd = lax.axis_index("dp"), lax.axis_index("hd")
    x, zh = lax.rem(hd, NX), lax.div(hd, NX)
    c, z, y = lax.rem(dp, 2), lax.rem(lax.div(dp, 2), NZ), lax.div(dp, 2 * NZ)
    o = 1 - c

    def at(x_=x, zh_=zh, y_=y, z_=z, c_=c):
        return ((y_ * NZ + z_) * 2 + c_, zh_ * NX + x_)

    def plus(v, d, n):
        return lax.rem(v + d, n)

    used = [0]
    sent = []

    def sems(n):
        first = used[0]
        used[0] += n
        return first

    def copy(src, dst, send, recv, dev):
        return pltpu.make_async_remote_copy(
            src_ref=src, dst_ref=dst, send_sem=ss.at[send], recv_sem=rs.at[recv],
            device_id=dev, device_id_type=MESH,
        )

    def go(src, dst, sem, dev):
        cp = copy(src, dst, sem, sem, dev)
        cp.start()
        sent.append((None, cp))
        return cp

    barrier = pltpu.get_barrier_semaphore()
    partners = [at(c_=o)]
    for d in range(1, 16):
        z16 = plus(zh * NZ + z, d, 16)
        partners.append(at(zh_=lax.div(z16, NZ), z_=lax.rem(z16, NZ)))
    for d in range(1, 16):
        partners.append(at(x_=plus(x, d % 4, NX), y_=plus(y, d // 4, NY)))
    for dev in partners:
        pl.semaphore_signal(barrier, inc=1, device_id=dev, device_id_type=MESH)

    count = counts[0]
    row16 = lax.broadcasted_iota(jnp.int32, (16, POS), 0)
    pos = lax.broadcasted_iota(jnp.int32, (16, POS), 1)
    for s in range(SLOTS):
        sc = lax.dot_general(query[s], cache[s], (((1,), (1,)), ((), ())), preferred_element_type=F32)
        sc = sc * F32(192.0**-0.5)
        keep = pos < lengths[s] - 1 + jnp.where(row16 >= HEADS, 1, 0)
        sc = jnp.where(keep, sc, -1e30)
        ex = jnp.exp(sc - jnp.max(sc, axis=-1, keepdims=True))
        wt = (ex / jnp.sum(ex, axis=-1, keepdims=True)).astype(BF16)
        la = jnp.dot(wt, cache[s, :, :LAT], preferred_element_type=F32)
        la = la.astype(BF16).astype(F32)
        for k in range(4):
            lat[k, pl.ds(s * 16, 16), :] = la[:, k * 128 : (k + 1) * 128]
    row8 = lax.broadcasted_iota(jnp.int32, (8, 128), 0)
    live = jnp.where(lax.div(row8, QTOK) < count, F32(1), F32(0))
    for h in range(HEADS):
        lh = [lat[k, pl.ds(h, 8, stride=HEADS), :] for k in range(4)]
        lh = jnp.concatenate(lh, axis=1).astype(BF16)
        hv = jnp.dot(lh, value_up[h], preferred_element_type=F32) * live
        hsc[h // 4, :, (h % 4) * 128 : (h % 4 + 1) * 128] = hv.astype(BF16).astype(F32)

    res, gain = residual[...].astype(F32), norm_gain[...]
    rsp[...] = jnp.zeros_like(rsp)
    gn[...] = jnp.zeros_like(gn)
    for b in range(8):
        lo = (b // 2) * 128
        rsp[b % 2, :, lo : lo + OUTCOL] = res[:, b * OUTCOL : (b + 1) * OUTCOL]
        gn[b % 2, :, lo : lo + OUTCOL] = gain[:, b * OUTCOL : (b + 1) * OUTCOL]

    pl.semaphore_wait(barrier, len(partners))

    peer = at(c_=o)
    heads_cp = go(hsc.at[o], tf.at[c], sems(1), peer)
    res_cp = go(rsp.at[o], rt.at[c], sems(1), peer)
    tf[c] = hsc[c]
    rt[c] = rsp[c]
    heads_cp.wait_recv()
    g1[c, y, z] = tf[...].reshape(16, 512).astype(BF16)

    def gather_z(g):
        first = sems(8)
        cps = {}
        for j in (7, 6, 5, 4, 3, 2, 1):
            cps[j] = go(g.at[c, y, z], g.at[c, y, z], first + j, at(z_=flip(z, j)))
        return cps

    def gather_rest(g, cps, consume):
        ysem, csem = sems(8), sems(8)
        zg = lax.div(z, 4) * 4
        ycp, ccp = {}, {}
        for gi in range(2):
            base = zg if gi == 0 else 4 - zg
            for j in range(gi * 4 + (gi == 0), gi * 4 + 4):
                cps[j].wait_recv()
            part = g.at[c, y, pl.ds(base, 4)]
            for d in (1, 3, 2):
                ycp[d, gi] = go(part, part, ysem + gi * 4 + d, at(y_=plus(y, d, NY)))
            ccp[0, gi] = go(part, part, csem + gi * 4, peer)
        for d in (1, 3, 2):
            yd = plus(y, NY - d, NY)
            for gi in range(2):
                ycp[d, gi].wait_recv()
                part = g.at[c, yd, pl.ds(zg if gi == 0 else 4 - zg, 4)]
                ccp[d, gi] = go(part, part, csem + gi * 4 + d, peer)
        for d in (0, 1, 3, 2):
            for gi in range(2):
                ccp[d, gi].wait_recv()
            consume(plus(y, NY - d, NY), d)

    cps = gather_z(g1)

    w1[...] = jnp.zeros_like(w1)
    w1[:, :OUTCOL] = out_proj[...]
    w2[...] = jnp.zeros_like(w2)
    for b in range(8):
        lo = (b // 2) * 128
        w2[b % 2, lo : lo + OUTCOL, :UNITS] = gate_w[b * OUTCOL : (b + 1) * OUTCOL, :]
        w2[b % 2, lo : lo + OUTCOL, UNITS : 2 * UNITS] = up_w[b * OUTCOL : (b + 1) * OUTCOL, :]
    r_ = lax.broadcasted_iota(jnp.int32, (16, 128), 0)
    c_ = lax.broadcasted_iota(jnp.int32, (16, 128), 1)
    ones = jnp.where((r_ < 2) & (c_ == 64), F32(1), F32(0)).astype(BF16)
    for k in range(2):
        w2[k, OUTCOL:128, 512:640] = ones
    w3[...] = jnp.zeros_like(w3)
    w3[0, :UNITS, :] = down_w[:, :512]
    w3[1, :UNITS, :384] = down_w[:, 512:]
    hb[...] = jnp.zeros_like(hb)

    xt = lax.rem(y, 2) * 2 + lax.div(z, 4)
    here = x == xt
    slot = lax.div(y, 2) * 4 + x
    psend, precv = sems(4), sems(8)
    slot_sem = precv + slot

    def out_projection(yd, d):
        left, right = g1[0, yd].reshape(128, 512), g1[1, yd].reshape(128, 512)
        pv = jnp.dot(left, w1[:512, :], preferred_element_type=F32)
        pv = pv + jnp.dot(right, w1[512:, :], preferred_element_type=F32)
        pb[yd] = pv.astype(BF16).reshape(NZ, 16, 128)
        cp = copy(pb.at[yd], rx.at[slot], psend + d, slot_sem, at(x_=xt, y_=yd))
        if d == 0:

            @pl.when(jnp.logical_not(here))
            def _():
                cp.start()

            @pl.when(here)
            def _():
                rx[slot] = pb[yd]

            sent.append((jnp.logical_not(here), cp))
        else:
            cp.start()
            sent.append((None, cp))

    gather_rest(g1, cps, out_projection)

    holder = lax.rem(x, 2) == lax.div(z, 4)
    own = jnp.logical_and(holder, lax.rem(y, 2) == lax.div(x, 2))
    zsend, zrecv = sems(16), sems(8)
    z16 = zh * NZ + z
    myslot = zh * 4 + lax.rem(z, 4)
    to_z = []
    for d in range(1, 16):
        t = plus(z16, d, 16)
        dev = at(zh_=lax.div(t, NZ), z_=lax.rem(t, NZ))
        to_z.append(copy(sb.at[t], rz.at[myslot], zsend + d, zrecv + myslot, dev))

    @pl.when(holder)
    def _():
        for i in range(8):
            is_self = jnp.logical_and(own, slot == i)

            @pl.when(jnp.logical_not(is_self))
            def _():
                copy(rx.at[i], rx.at[i], psend, precv + i, peer).wait_recv()

        for k in range(2):
            tot = rx[4 * k].astype(F32) + rx[4 * k + 1].astype(F32)
            tot = tot + rx[4 * k + 2].astype(F32) + rx[4 * k + 3].astype(F32)
            sb[pl.ds(8 * k, 8)] = tot.astype(BF16)
        rz[myslot] = sb[z16]
        for cp in to_z:
            cp.start()

    for cp in to_z:
        sent.append((holder, cp))
    for i in range(8):
        is_self = jnp.logical_and(holder, myslot == i)

        @pl.when(jnp.logical_not(is_self))
        def _():
            copy(rz.at[i], rz.at[i], zsend, zrecv + i, peer).wait_recv()

    res_cp.wait_recv()
    tiles = []
    for b in range(4):
        attn = (rz[b].astype(F32) + rz[4 + b].astype(F32)).astype(BF16).astype(F32)
        tiles.append(attn)
    attn = jnp.concatenate(tiles, axis=1)
    state = (rt[...].reshape(16, 512) + attn).astype(BF16).astype(F32)
    square = jnp.sum(state * state, axis=1, keepdims=True)
    high = square.astype(BF16).astype(F32)
    low = square - high
    scaled = state * gn[c]
    lane = lax.broadcasted_iota(jnp.int32, (16, 512), 1)
    scaled = jnp.where(lane == OUTCOL, high, jnp.where(lane == OUTCOL + 1, low, scaled))
    g2[c, y, z] = scaled.astype(BF16)
    cps = gather_z(g2)
    st[...] = state.reshape(2, 8, 512)
    st_cp = go(st.at[o], so.at[c], sems(1), peer)
    so[c] = st[c]

    gsem = sems(16)
    gcp = {}

    def gate_up(yd, d):
        left, right = g2[0, yd].reshape(128, 512), g2[1, yd].reshape(128, 512)
        gu = jnp.dot(left, w2[0], preferred_element_type=F32)
        gu = gu + jnp.dot(right, w2[1], preferred_element_type=F32)
        gb[d] = gu.astype(BF16).reshape(NX, 32, 640)
        for e in (1, 3, 2):
            xd = plus(x, e, NX)
            gcp[d, e] = go(gb.at[d, xd], rxg.at[d, e - 1], gsem + d * 4 + e, at(x_=xd))

    gather_rest(g2, cps, gate_up)

    hsem = sems(4)
    other = at(zh_=1 - zh)
    order = (0, 1, 3, 2)
    hcp = {}
    for d in order:
        tot = gb[d, x].astype(F32)
        for e in (1, 3, 2):
            gcp[d, e].wait_recv()
            tot = tot + rxg[d, e - 1].astype(F32)
        sx[d] = tot.astype(BF16)
        hcp[d] = go(sx.at[d], rzh.at[d], hsem + d, other)

    asem = sems(16)
    acp = {}
    for d in order:
        hcp[d].wait_recv()
        gu = sx[d].astype(F32) + rzh[d].astype(F32)
        inv = lax.rsqrt(gu[:, 2 * UNITS : 2 * UNITS + 1] / D + 1e-06)
        gate, up = gu[:, :UNITS] * inv, gu[:, UNITS : 2 * UNITS] * inv
        hid = gate / (1.0 + jnp.exp(-gate)) * up
        hb[d, x, :, :UNITS] = hid.astype(BF16)
        for e in (1, 3, 2):
            acp[d, e] = go(hb.at[d, x], hb.at[d, x], asem + d * 4 + e, at(x_=plus(x, e, NX)))

    dsem = sems(4)
    dcp = {}
    for d in order:
        for e in (1, 3, 2):
            acp[d, e].wait_recv()
        hidden = hb[d].reshape(128, 384)
        there = jnp.dot(hidden, w3[o], preferred_element_type=F32)
        dsend[d] = there.astype(BF16)
        dcp[d] = go(dsend.at[d], drecv.at[d], dsem + d, peer)

    fsem = sems(4)
    fcp = {}
    mine = None
    for d in (1, 3, 2, 0):
        part = jnp.dot(hb[d].reshape(128, 384), w3[c], preferred_element_type=F32)
        dcp[d].wait_recv()
        part = part + drecv[d].astype(F32)
        if d == 0:
            mine = part
        else:
            eb[d - 1] = part.astype(BF16)
            fcp[d] = go(eb.at[d - 1], fr.at[d - 1], fsem + d, at(y_=plus(y, NY - d, NY)))

    st_cp.wait_recv()
    for b in range(8):
        lo = (b // 2) * 128
        stf[:, b * OUTCOL : (b + 1) * OUTCOL] = so[b % 2, :, lo : lo + OUTCOL]

    for d in (1, 3, 2):
        fcp[d].wait_recv()
        mine = mine + fr[d - 1].astype(F32)
    fb[...] = mine.astype(BF16).reshape(NZ, 16, 512)
    osem = sems(8)
    ocp = {}
    for j in (7, 6, 5, 4, 3, 2, 1):
        t = flip(z, j)
        ocp[j] = go(fb.at[t], zr.at[j], osem + j, at(z_=t))
    tot = fb[z].astype(F32)
    for j in range(1, 8):
        ocp[j].wait_recv()
        tot = tot + zr[j].astype(F32)
    osum[...] = tot.reshape(2, 8, 512)
    last = go(osum.at[o], orx.at[c], sems(1), peer)
    orx[c] = osum[c]
    last.wait_recv()
    livew = live[:, :1]
    out[:, :512] = ((stf[:, :512] + orx[0]) * livew).astype(BF16)
    out[:, 512:] = ((stf[:, 512:] + orx[1, :, :384]) * livew).astype(BF16)

    for when, cp in sent:
        if when is None:
            cp.wait_send()
        else:
            pl.when(when)(cp.wait_send)
    assert used[0] <= NSEM


def per_device(query, cache, lengths, counts, value_up, out_proj, residual, norm_gain, gate_w, up_w, down_w):
    vmem, smem = pl.BlockSpec(memory_space=pltpu.VMEM), pl.BlockSpec(memory_space=pltpu.SMEM)
    b, f = lambda *s: pltpu.VMEM(s, BF16), lambda *s: pltpu.VMEM(s, F32)
    return pl.pallas_call(
        kernel,
        out_shape=jax.ShapeDtypeStruct((8, FEAT), BF16),
        in_specs=[vmem, vmem, smem, smem] + [vmem] * 7,
        out_specs=vmem,
        scratch_shapes=[
            f(4, 64, 128), f(2, 8, 512), f(2, 8, 512), b(2, NY, NZ, 16, 512), b(1024, 128),
            b(NY, NZ, 16, 128), b(8, NZ, 16, 128), b(16, 16, 128), b(8, 16, 128),
            f(2, 8, 512), f(2, 8, 512), f(2, 1, 512), f(2, 8, 512), f(2, 8, 512),
            b(2, NY, NZ, 16, 512), b(2, 512, 640), b(NY, NX, 32, 640), b(NY, 3, 32, 640),
            b(NY, 32, 640), b(NY, 32, 640), b(NY, NX, 32, 384), b(2, 384, 512),
            b(NY, 128, 512), b(NY, 128, 512), b(3, 128, 512), b(3, 128, 512),
            b(NZ, 16, 512), b(NZ, 16, 512), f(2, 8, 512), f(2, 8, 512), f(8, FEAT),
            pltpu.SemaphoreType.DMA((NSEM,)), pltpu.SemaphoreType.DMA((NSEM,)),
        ],
        compiler_params=pltpu.CompilerParams(
            collective_id=0, has_side_effects=True, vmem_limit_bytes=48 << 20
        ),
        name="decode_layer",
    )(
        query.reshape(SLOTS, QTOK * HEADS, QK), cache, lengths, counts, value_up, out_proj, residual,
        norm_gain.reshape(1, FEAT), gate_w, up_w, down_w,
    )


def solution(mesh):
    return jax.shard_map(
        per_device,
        mesh=mesh,
        in_specs=(
            P("dp", None, "hd", None), P("dp", None, None), P("dp"), P("dp"), P("hd", None, None), P("hd", "dp"),
            P("dp", "hd"), P("hd"), P("hd", "dp"), P("hd", "dp"), P("dp", "hd"),
        ),
        out_specs=P("dp", "hd"),
        check_vma=False,
    )
```

time: 1390 us -> 121 us (0.09)
  waiting for transfers between devices: 1170 us -> 0 us
  blocking collectives: 186 us -> 0 us
  Pallas kernels: 0 us -> 113 us
    unnamed x5 -> x0, waiting for transfers between devices: 822 us -> none
    psum x1 -> x0, waiting for transfers between devices: 131 us -> none  [per_device(): gate_sum, up_sum, total_sq = lax.psum((gate_part, up_part, sumsq), 'hd')]
    all_gather x1 -> x0, waiting for transfers between devices: 125 us -> none  [per_device(): lax.all_gather(head_out, 'dp', axis=0, tiled=True)]
    all_gather x1 -> x0, blocking collectives: 121 us -> none  [per_device(): gathered = lax.all_gather(state, 'dp', axis=0, tiled=True)]
    pallas_call x0 -> x1, Pallas kernels: none -> 113 us  [per_device(): pl.pallas_call(kernel, out_shape=jax.ShapeDtypeStruct((8, FEAT), BF16), i...]
    reduce_scatter x1 -> x0, waiting for transfers between devices: 95.5 us -> none  [per_device(): attn = lax.psum_scatter(moved, 'hd', scatter_dimension=1, tiled=True)]
    psum x1 -> x0, blocking collectives: 39 us -> none  [per_device(): gate_sum, up_sum, total_sq = lax.psum((gate_part, up_part, sumsq), 'hd')]
    all_to_all x1 -> x0, blocking collectives: 26.4 us -> none  [per_device(): lax.all_to_all(partial_value, 'dp', split_axis=0, concat_axis=1, tiled=True)]
  transfers between devices with their start and end apart: 4 -> 0, of which waited for: 4 -> 0; matrix products, arithmetic and copies ran while one was open for 0% -> 0% of each run, Pallas kernels for 0% -> 0%
where the time goes in v1:
time: 121 us; the launch traced here: 120 us
  Pallas kernels  113 us (93%)
  local copies, waits for them, and re-layouts  6.57 us (5%)
    pallas_call x1, Pallas kernels, per_device(): pl.pallas_call(kernel, out_shape=jax.ShapeDtypeStruct((8, FEAT), BF16), i...  113 us
    unnamed x16, local copies, waits for them, and re-layouts  5.88 us

profile of v1, /device:TPU:1, one launch (start us, length us, event | category | flops | bytes accessed | tf_op | source)
XLA Modules:
  0.0 120.3 jit_solution(304089952118322042)
XLA Ops:
  0.7 0.7 reshape.7.norm_gain
  1.3 1.1 copy.12.out_proj
  2.5 0.0 copy-start
  2.5 1.5 %copy.13.gate_w = bf16[896,288]{1,0:T(8,128)(2,1)S(1)} copy(bf16[896,288]{0,1:T(8,128)(2,1)} %param.19) | data formatting | bytes 1032192 | tf_op args[8]
  4.0 0.0 copy-start.2
  4.0 0.0 copy-start.3
  4.0 0.0 copy-start.4
  4.0 0.0 copy-start.5
  4.0 1.5 %copy.14.up_w = bf16[896,288]{1,0:T(8,128)(2,1)S(1)} copy(bf16[896,288]{0,1:T(8,128)(2,1)} %param.20) | data formatting | bytes 1032192 | tf_op args[9]
  5.5 0.0 copy-done
  5.5 0.0 copy-done.2
  5.5 0.0 copy-done.3
  5.5 0.0 copy-done.4
  5.5 0.0 copy-done.5
  5.5 0.0 copy-start.1
  5.5 1.2 copy-done.1
  6.7 113.0 %decode_layer.1 = bf16[8,896]{1,0:T(8,128)(2,1)S(1)} custom-call(bf16[4,16,576]{2,1,0:T(8,128)(2,1)S(1)} %bitcast.1, bf16[4,192,576]{2,1,0:T(8,128)(2,1)S(1)} %copy-done.1, s32[4]{0:T(128)S(1)} %copy-done.5, s32[1]{0:T(128)S(6)} %copy.16.counts, bf16[8,512,128]{2,1,0:T(8,128)(2,1)S(1)} %copy-done, bf16[1024,112]{1,0:T(8,128)(2,1)S(1)} %copy.12.out_proj, ...), custom_call_target="tpu_custom_call" | custom-call | tf_op jit(solution)/shard_map/decode_layer/pallas_call | solution.py:345
  119.7 0.6 copy.17
Async XLA Ops:
  2.5 3.0 %copy-start = (bf16[8,512,128]{2,1,0:T(8,128)(2,1)S(1)}, bf16[8,512,128]{2,1,0:T(8,128)(2,1)}, u32[]{:S(2)}) copy-start(bf16[8,512,128]{2,1,0:T(8,128)(2,1)} %value_up.1) | copy-start | bytes 3145732
  4.0 1.5 %copy-start.2 = (bf16[288,896]{1,0:T(8,128)(2,1)S(1)}, bf16[288,896]{1,0:T(8,128)(2,1)}, u32[]{:S(2)}) copy-start(bf16[288,896]{1,0:T(8,128)(2,1)} %down_w.1) | copy-start | bytes 1548292
  4.0 1.5 %copy-start.3 = (bf16[4,2,8,576]{3,2,1,0:T(8,128)(2,1)S(1)}, bf16[4,2,8,576]{3,2,1,0:T(8,128)(2,1)}, u32[]{:S(2)}) copy-start(bf16[4,2,8,576]{3,2,1,0:T(8,128)(2,1)} %param.11) | copy-start | bytes 221188
  4.0 1.5 %copy-start.4 = (bf16[8,896]{1,0:T(8,128)(2,1)S(1)}, bf16[8,896]{1,0:T(8,128)(2,1)}, u32[]{:S(2)}) copy-start(bf16[8,896]{1,0:T(8,128)(2,1)} %residual.1) | copy-start | bytes 43012
  4.0 1.5 %copy-start.5 = (s32[4]{0:T(128)S(1)}, s32[4]{0:T(128)}, u32[]{:S(2)}) copy-start(s32[4]{0:T(128)} %lengths.1) | copy-start | bytes 52
  5.5 1.2 %copy-start.1 = (bf16[4,192,576]{2,1,0:T(8,128)(2,1)S(1)}, bf16[4,192,576]{2,1,0:T(8,128)(2,1)}, u32[]{:S(2)}) copy-start(bf16[4,192,576]{2,1,0:T(8,128)(2,1)} %cache.1) | copy-start | bytes 2654212

commit v2 on v1

v2 whole, which is shorter than its diff:
```python
import functools

import jax
import jax.numpy as jnp
from jax import lax
from jax.experimental import pallas as pl
from jax.experimental.pallas import tpu as pltpu
from jax.sharding import PartitionSpec as P

MESH = pl.DeviceIdType.MESH
F32, BF16 = jnp.float32, jnp.bfloat16
D = 7168
SLOTS, QTOK, HEADS, LAT, QK, POS = 4, 2, 8, 512, 576, 192
NX, NY, NZ, NSEM = 4, 4, 8, 72
OUTCOL, FEAT, UNITS = 112, 896, 288


def flip(value, mask, bits=3):
    out = 0
    for i in range(bits):
        bit = lax.rem(lax.div(value, 1 << i), 2)
        out = out + (1 - bit if (mask >> i) & 1 else bit) * (1 << i)
    return out


def dot_t(a, b):
    return lax.dot_general(a, b, (((1,), (1,)), ((), ())), preferred_element_type=F32)


def kernel(
    query_h, cache_h, lengths_h, counts_h, value_h, proj_h, res_h, gain_h, gate_h, up_h, down_h,
    out,
    query, cache, lengths, counts, value_up, out_proj, residual, norm_gain, gate_w, up_w, down_w, ls,
    lat, hsc, tf, g1, w1, pb, rx, sb, rz, rsp, rt, gn, st, so, g2, w2, gb, rxg, sx, rzh, hb, w3,
    dsend, drecv, eb, fr, fb, zr, osum, orx, stf, acc, ss,
):
    dp, hd = lax.axis_index("dp"), lax.axis_index("hd")
    x, zh = lax.rem(hd, NX), lax.div(hd, NX)
    c, z, y = lax.rem(dp, 2), lax.rem(lax.div(dp, 2), NZ), lax.div(dp, 2 * NZ)
    o = 1 - c

    def at(x_=x, zh_=zh, y_=y, z_=z, c_=c):
        return ((y_ * NZ + z_) * 2 + c_, zh_ * NX + x_)

    def plus(v, d, n):
        return lax.rem(v + d, n)

    used = [0]
    ends = []

    def sems(n):
        first = used[0]
        used[0] += n
        return first

    def copy(src, dst, send, recv, dev):
        return pltpu.make_async_remote_copy(
            src_ref=src, dst_ref=dst, send_sem=ss.at[send], recv_sem=ss.at[recv],
            device_id=dev, device_id_type=MESH,
        )

    def go(src, dst, send, recv, dev):
        copy(src, dst, send, recv, dev).start()

    def arrive(ref, recv):
        copy(ref, ref, recv, recv, peer).wait_recv()

    def sending(ref, when=None):
        send = sems(1)
        ends.append((when, ref, send))
        return send

    barrier = pltpu.get_barrier_semaphore()
    peer = at(c_=o)
    partners = [peer]
    for d in range(1, 16):
        z16 = plus(zh * NZ + z, d, 16)
        partners.append(at(zh_=lax.div(z16, NZ), z_=lax.rem(z16, NZ)))
    for d in range(1, 16):
        partners.append(at(x_=plus(x, d % 4, NX), y_=plus(y, d // 4, NY)))
    for dev in partners:
        pl.semaphore_signal(barrier, inc=1, device_id=dev, device_id_type=MESH)

    loads = {}
    pairs = (
        (query_h, query), (cache_h, cache), (value_h, value_up), (res_h, residual), (gain_h, norm_gain),
        (proj_h, out_proj), (gate_h, gate_w), (up_h, up_w), (down_h, down_w), (lengths_h, lengths), (counts_h, counts),
    )
    for i, (src, dst) in enumerate(pairs):
        loads[i] = pltpu.make_async_copy(src, dst, ls.at[i])
        loads[i].start()

    loads[9].wait()
    row = lax.broadcasted_iota(jnp.int32, (64, POS), 0)
    pos = lax.broadcasted_iota(jnp.int32, (64, POS), 1)
    limit = lax.rem(lax.div(row, HEADS), QTOK) - 1
    for i in range(SLOTS):
        limit = limit + jnp.where(lax.div(row, 16) == i, lengths[i], 0)
    loads[0].wait()
    loads[1].wait()
    sc = [dot_t(query[i], cache[i]) for i in range(SLOTS)]
    sc = jnp.concatenate(sc, axis=0) * F32(192.0**-0.5)
    sc = jnp.where(pos < limit, sc, -1e30)
    ex = jnp.exp(sc - jnp.max(sc, axis=-1, keepdims=True))
    wt = (ex / jnp.sum(ex, axis=-1, keepdims=True)).astype(BF16)
    for i in range(SLOTS):
        la = jnp.dot(wt[16 * i : 16 * i + 16], cache[i, :, :LAT], preferred_element_type=F32)
        la = la.astype(BF16).astype(F32)
        for k in range(4):
            lat[k, pl.ds(i * 16, 16), :] = la[:, k * 128 : (k + 1) * 128]
    loads[2].wait()
    loads[10].wait()
    count = counts[0]
    row8 = lax.broadcasted_iota(jnp.int32, (8, 128), 0)
    live = jnp.where(lax.div(row8, QTOK) < count, F32(1), F32(0))
    for h in range(HEADS):
        lh = [lat[k, pl.ds(h, 8, stride=HEADS), :] for k in range(4)]
        lh = jnp.concatenate(lh, axis=1).astype(BF16)
        hv = jnp.dot(lh, value_up[h], preferred_element_type=F32) * live
        hsc[h // 4, :, (h % 4) * 128 : (h % 4 + 1) * 128] = hv.astype(BF16).astype(F32)

    loads[3].wait()
    loads[4].wait()
    res = residual[...].astype(F32)
    gain = jnp.concatenate([norm_gain[i : i + 1, :] for i in range(7)], axis=1)
    rsp[...] = jnp.zeros_like(rsp)
    gn[...] = jnp.zeros_like(gn)
    for b in range(8):
        lo = (b // 2) * 128
        rsp[b % 2, :, lo : lo + OUTCOL] = res[:, b * OUTCOL : (b + 1) * OUTCOL]
        gn[b % 2, :, lo : lo + OUTCOL] = gain[:, b * OUTCOL : (b + 1) * OUTCOL]

    w1[...] = jnp.zeros_like(w1)
    loads[5].wait()
    w1[:OUTCOL, :] = out_proj[...]

    pl.semaphore_wait(barrier, len(partners))

    heads_in, res_in = sems(1), sems(1)
    go(hsc.at[o], tf.at[c], sending(hsc.at[0]), heads_in, peer)
    go(rsp.at[o], rt.at[c], sending(rsp.at[0]), res_in, peer)
    tf[c] = hsc[c]
    rt[c] = rsp[c]
    arrive(tf.at[c], heads_in)
    g1[c, y, z] = tf[...].reshape(16, 512).astype(BF16)

    def gather_z(g):
        send, recv = sending(g.at[0, 0, pl.ds(0, 7)]), sems(2)
        for j in (7, 6, 5, 4, 3, 2, 1):
            go(g.at[c, y, z], g.at[c, y, z], send, recv + j // 4, at(z_=flip(z, j)))
        return recv

    def gather_y(g, zrecv, consume):
        ysend, csend, yrecv, crecv = sending(g.at[0, pl.ds(0, 3)]), sending(g.at[0]), sems(8), sems(4)
        near = lax.div(z, 4) * 4
        base = (near, 4 - near)
        for gi in range(2):
            arrive(g.at[c, y, pl.ds(base[gi], 3 + gi)], zrecv + gi)
            part = g.at[c, y, pl.ds(base[gi], 4)]
            for d in (2, 1, 3):
                go(part, part, ysend, yrecv + gi * 4 + d, at(y_=plus(y, d, NY)))
            go(part, part, csend, crecv, peer)

        def forward(d):
            yd = plus(y, NY - d, NY)
            for gi in range(2):
                part = g.at[c, yd, pl.ds(base[gi], 4)]
                arrive(part, yrecv + gi * 4 + d)
                go(part, part, csend, crecv + d, peer)

        def take(d):
            yd = plus(y, NY - d, NY)
            arrive(g.at[o, yd], crecv + d)
            consume(yd, d)

        return forward, take

    cps = gather_z(g1)

    w2[...] = jnp.zeros_like(w2)
    loads[6].wait()
    loads[7].wait()
    for b in range(8):
        lo = (b // 2) * 128
        w2[b % 2, :UNITS, lo : lo + OUTCOL] = gate_w[:, b * OUTCOL : (b + 1) * OUTCOL]
        w2[b % 2, UNITS : 2 * UNITS, lo : lo + OUTCOL] = up_w[:, b * OUTCOL : (b + 1) * OUTCOL]
    r_ = lax.broadcasted_iota(jnp.int32, (16, 128), 0)
    c_ = lax.broadcasted_iota(jnp.int32, (16, 128), 1)
    ones = jnp.where((r_ == 0) & (c_ >= OUTCOL) & (c_ < OUTCOL + 2), F32(1), F32(0)).astype(BF16)
    for k in range(2):
        w2[k, 2 * UNITS : 2 * UNITS + 16, :128] = ones
    hb[...] = jnp.zeros_like(hb)

    xt = lax.rem(y, 2) * 2 + lax.div(z, 4)
    here = x == xt
    slot = lax.div(y, 2) * 4 + x
    psend, pself, precv = sending(pb.at[pl.ds(0, 3)]), sending(pb.at[0], jnp.logical_not(here)), sems(2)

    def out_projection(yd, d):
        left, right = g1[0, yd].reshape(128, 512), g1[1, yd].reshape(128, 512)
        pv = dot_t(left, w1[:, :512]) + dot_t(right, w1[:, 512:])
        pb[yd] = pv.astype(BF16).reshape(NZ, 16, 128)
        cp = copy(pb.at[yd], rx.at[slot], psend if d else pself, precv + lax.div(y, 2), at(x_=xt, y_=yd))
        if d:
            cp.start()
        else:
            pl.when(jnp.logical_not(here))(cp.start)

            @pl.when(here)
            def _():
                rx[slot] = pb[yd]

    forward, take = gather_y(g1, cps, out_projection)
    take(0)
    forward(1)
    forward(3)
    take(1)
    forward(2)
    take(3)
    take(2)

    holder = lax.rem(x, 2) == lax.div(z, 4)
    own = jnp.logical_and(holder, lax.rem(y, 2) == lax.div(x, 2))
    zsend, zrecv = sending(sb.at[pl.ds(0, 15)], holder), sems(1)
    z16 = zh * NZ + z
    myslot = zh * 4 + lax.rem(z, 4)

    for k in (1 - zh, zh):

        @pl.when(holder)
        def _():
            is_self = jnp.logical_and(own, lax.div(y, 2) == k)
            pl.when(is_self)(lambda: arrive(rx.at[pl.ds(0, 3)], precv + k))
            pl.when(jnp.logical_not(is_self))(lambda: arrive(rx.at[pl.ds(0, 4)], precv + k))
            tot = rx[4 * k].astype(F32) + rx[4 * k + 1].astype(F32)
            tot = tot + rx[4 * k + 2].astype(F32) + rx[4 * k + 3].astype(F32)
            sb[pl.ds(8 * k, 8)] = tot.astype(BF16)
            for d in (4, 3, 5, 2, 6, 1, 7, 0):
                zd = plus(z, d, NZ)
                cp = copy(sb.at[8 * k + zd], rz.at[myslot], zsend, zrecv, at(zh_=k, z_=zd))
                if d:
                    cp.start()
                else:
                    pl.when(k != zh)(cp.start)

    @pl.when(holder)
    def _():
        rz[myslot] = sb[z16]

    w3[...] = jnp.zeros_like(w3)
    loads[8].wait()
    w3[0, :UNITS, :] = down_w[:, :512]
    w3[1, :UNITS, :384] = down_w[:, 512:]
    pl.when(holder)(lambda: arrive(rz.at[pl.ds(0, 7)], zrecv))
    pl.when(jnp.logical_not(holder))(lambda: arrive(rz, zrecv))

    arrive(rt.at[c], res_in)
    tiles = []
    for b in range(4):
        attn = (rz[b].astype(F32) + rz[4 + b].astype(F32)).astype(BF16).astype(F32)
        tiles.append(attn)
    attn = jnp.concatenate(tiles, axis=1)
    state = (rt[...].reshape(16, 512) + attn).astype(BF16).astype(F32)
    square = jnp.sum(state * state, axis=1, keepdims=True)
    high = square.astype(BF16).astype(F32)
    low = square - high
    scaled = state * gn[c]
    lane = lax.broadcasted_iota(jnp.int32, (16, 512), 1)
    scaled = jnp.where(lane == OUTCOL, high, jnp.where(lane == OUTCOL + 1, low, scaled))
    g2[c, y, z] = scaled.astype(BF16)
    cps = gather_z(g2)
    st[...] = state.reshape(2, 8, 512)
    st_in = sems(1)
    go(st.at[o], so.at[c], sending(st.at[0]), st_in, peer)
    so[c] = st[c]

    gsend, grecv = sending(gb.at[pl.ds(0, 3)]), sems(4)

    def gate_up(yd, d):
        left, right = g2[0, yd].reshape(128, 512), g2[1, yd].reshape(128, 512)
        gu = dot_t(left, w2[0]) + dot_t(right, w2[1])
        gb[d] = gu.astype(BF16).reshape(NX, 32, 640)
        for e in (1, 3, 2):
            xd = plus(x, e, NX)
            go(gb.at[d, xd], rxg.at[d, e - 1], gsend, grecv + d, at(x_=xd))

    hsend, hrecv = sending(sx), sems(4)
    other = at(zh_=1 - zh)

    def sum_x(d):
        tot = gb[d, x].astype(F32)
        arrive(rxg.at[d], grecv + d)
        for e in (1, 3, 2):
            tot = tot + rxg[d, e - 1].astype(F32)
        sx[d] = tot.astype(BF16)
        go(sx.at[d], rzh.at[d], hsend, hrecv + d, other)

    asend, arecv = sending(hb.at[pl.ds(0, 3)]), sems(4)

    def hidden_units(d):
        arrive(rzh.at[d], hrecv + d)
        gu = sx[d].astype(F32) + rzh[d].astype(F32)
        inv = lax.rsqrt(gu[:, 2 * UNITS : 2 * UNITS + 1] / D + 1e-06)
        gate, up = gu[:, :UNITS] * inv, gu[:, UNITS : 2 * UNITS] * inv
        hid = gate / (1.0 + jnp.exp(-gate)) * up
        hb[d, x, :, :UNITS] = hid.astype(BF16)
        for e in (1, 3, 2):
            go(hb.at[d, x], hb.at[d, x], asend, arecv + d, at(x_=plus(x, e, NX)))

    dout, din = sending(dsend), sems(4)

    def down_there(d):
        arrive(hb.at[d, pl.ds(0, 3)], arecv + d)
        there = jnp.dot(hb[d].reshape(128, 384), w3[o], preferred_element_type=F32)
        dsend[d] = there.astype(BF16)
        go(dsend.at[d], drecv.at[d], dout, din + d, peer)

    fsend, frecv = sending(eb), sems(1)

    def down_here(d):
        part = jnp.dot(hb[d].reshape(128, 384), w3[c], preferred_element_type=F32)
        arrive(drecv.at[d], din + d)
        part = part + drecv[d].astype(F32)
        if d == 0:
            acc[...] = part.reshape(NZ, 16, 512)
        else:
            eb[d - 1] = part.astype(BF16).reshape(NZ, 16, 512)
            go(eb.at[d - 1], fr.at[d - 1], fsend, frecv, at(y_=plus(y, NY - d, NY)))

    forward, take = gather_y(g2, cps, gate_up)
    take(0)
    forward(1)
    forward(3)
    take(1)
    sum_x(0)
    forward(2)
    take(3)
    take(2)
    sum_x(1)
    sum_x(3)
    sum_x(2)
    hidden_units(0)
    down_there(0)
    hidden_units(1)
    hidden_units(3)
    down_here(0)
    hidden_units(2)
    down_there(1)
    down_there(3)
    down_here(1)
    down_here(3)
    down_there(2)
    down_here(2)

    arrive(so.at[c], st_in)
    for b in range(8):
        lo = (b // 2) * 128
        stf[:, b * OUTCOL : (b + 1) * OUTCOL] = so[b % 2, :, lo : lo + OUTCOL]

    arrive(fr, frecv)
    oout, oin = sending(fb.at[pl.ds(0, 7)]), sems(1)

    def sum_y(t):
        return acc[t] + fr[0, t].astype(F32) + fr[1, t].astype(F32) + fr[2, t].astype(F32)

    for j in (7, 6, 5, 4, 3, 2, 1):
        t = flip(z, j)
        fb[t] = sum_y(t).astype(BF16)
        go(fb.at[t], zr.at[j - 1], oout, oin, at(z_=t))
    tot = sum_y(z)
    arrive(zr, oin)
    for j in range(7):
        tot = tot + zr[j].astype(F32)
    osum[...] = tot.reshape(2, 8, 512)
    last = sems(1)
    go(osum.at[o], orx.at[c], sending(osum.at[0]), last, peer)
    orx[c] = osum[c]
    arrive(orx.at[c], last)
    livew = live[:, :1]
    out[:, :512] = ((stf[:, :512] + orx[0]) * livew).astype(BF16)
    out[:, 512:] = ((stf[:, 512:] + orx[1, :, :384]) * livew).astype(BF16)

    for when, ref, send in ends:
        if when is None:
            copy(ref, ref, send, send, peer).wait_send()
        else:
            pl.when(when)(lambda ref=ref, send=send: copy(ref, ref, send, send, peer).wait_send())
    assert used[0] == NSEM, used


def per_device(query, cache, lengths, counts, value_up, out_proj, residual, norm_gain, gate_w, up_w, down_w):
    hbm = pl.BlockSpec(memory_space=pltpu.HBM)
    vmem = pl.BlockSpec(memory_space=pltpu.VMEM)
    b, f = lambda *s: pltpu.VMEM(s, BF16), lambda *s: pltpu.VMEM(s, F32)
    return pl.pallas_call(
        kernel,
        out_shape=jax.ShapeDtypeStruct((8, FEAT), BF16),
        in_specs=[hbm] * 11,
        out_specs=vmem,
        scratch_shapes=[
            b(SLOTS, 16, QK), b(SLOTS, POS, QK), pltpu.SMEM((4,), jnp.int32), pltpu.SMEM((1,), jnp.int32), b(HEADS, LAT, 128), b(OUTCOL, 1024), b(8, FEAT), f(7, 128),
            b(UNITS, FEAT), b(UNITS, FEAT), b(UNITS, FEAT), pltpu.SemaphoreType.DMA((11,)),
            f(4, 64, 128), f(2, 8, 512), f(2, 8, 512), b(2, NY, NZ, 16, 512), b(128, 1024),
            b(NY, NZ, 16, 128), b(8, NZ, 16, 128), b(16, 16, 128), b(8, 16, 128),
            f(2, 8, 512), f(2, 8, 512), f(2, 1, 512), f(2, 8, 512), f(2, 8, 512),
            b(2, NY, NZ, 16, 512), b(2, 640, 512), b(NY, NX, 32, 640), b(NY, 3, 32, 640),
            b(NY, 32, 640), b(NY, 32, 640), b(NY, NX, 32, 384), b(2, 384, 512),
            b(NY, 128, 512), b(NY, 128, 512), b(3, NZ, 16, 512), b(3, NZ, 16, 512),
            b(NZ, 16, 512), b(7, 16, 512), f(2, 8, 512), f(2, 8, 512), f(8, FEAT), f(NZ, 16, 512),
            pltpu.SemaphoreType.DMA((NSEM,)),
        ],
        compiler_params=pltpu.CompilerParams(
            collective_id=0, has_side_effects=True, vmem_limit_bytes=60 << 20
        ),
        name="decode_layer",
    )(
        query.reshape(SLOTS, QTOK * HEADS, QK), cache, lengths, counts, value_up, out_proj.T, residual,
        norm_gain.reshape(7, 128), gate_w.T, up_w.T, down_w,
    )


def solution(mesh):
    return jax.shard_map(
        per_device,
        mesh=mesh,
        in_specs=(
            P("dp", None, "hd", None), P("dp", None, None), P("dp"), P("dp"), P("hd", None, None), P("hd", "dp"),
            P("dp", "hd"), P("hd"), P("hd", "dp"), P("hd", "dp"), P("dp", "hd"),
        ),
        out_specs=P("dp", "hd"),
        check_vma=False,
    )
```

time: 121 us -> 109 us (0.901)
  Pallas kernels: 113 us -> 107 us
  local copies, waits for them, and re-layouts: 6.57 us -> 1.31 us
    pallas_call x1, Pallas kernels: 113 us -> 107 us  [per_device(): pl.pallas_call(kernel, out_shape=jax.ShapeDtypeStruct((8, FEAT), BF16), i...]
    unnamed x16 -> x1, local copies, waits for them, and re-layouts: 5.88 us -> 1.31 us
where the time goes in v2:
time: 109 us
  Pallas kernels  107 us (98%)
  local copies, waits for them, and re-layouts  1.31 us (1%)
    pallas_call x1, Pallas kernels, per_device(): pl.pallas_call(kernel, out_shape=jax.ShapeDtypeStruct((8, FEAT), BF16), i...  107 us

profile of v2, /device:TPU:1, one launch (start us, length us, event | category | flops | bytes accessed | tf_op | source)
XLA Modules:
  0.0 108.6 jit_solution(11673912544608045224)
XLA Ops:
  0.7 106.6 %decode_layer.1 = bf16[8,896]{1,0:T(8,128)(2,1)} custom-call(bf16[4,16,576]{2,1,0:T(8,128)(2,1)} %bitcast.8, bf16[4,192,576]{2,1,0:T(8,128)(2,1)} %cache_h.1, s32[4]{0:T(128)} %lengths_h.1, s32[1]{0:T(128)S(6)} %copy.13.counts_h, bf16[8,512,128]{2,1,0:T(8,128)(2,1)} %value_h.1, bf16[112,1024]{1,0:T(8,128)(2,1)} %bitcast.7, bf16[8,896]{1,0:T(8,128)(2,1)} %res_h.1, ...), custom_call_target="tpu_custom_call" | custom-call | tf_op jit(solution)/shard_map/decode_layer/pallas_call | solution.py:395
  107.3 1.3 %copy.14 = bf16[8,896]{1,0:T(8,128)(2,1)} copy(bf16[8,896]{1,0:T(8,128)(2,1)} %decode_layer.1) | data formatting | bytes 28672

commit v3 on v2

--- a/solution.py
+++ b/solution.py
@@ -31,8 +31,8 @@
     query_h, cache_h, lengths_h, counts_h, value_h, proj_h, res_h, gain_h, gate_h, up_h, down_h,
     out,
     query, cache, lengths, counts, value_up, out_proj, residual, norm_gain, gate_w, up_w, down_w, ls,
-    lat, hsc, tf, g1, w1, pb, rx, sb, rz, rsp, rt, gn, st, so, g2, w2, gb, rxg, sx, rzh, hb, w3,
-    dsend, drecv, eb, fr, fb, zr, osum, orx, stf, acc, ss,
+    lat, hsc, g1, w1, pb, rx, sb, rz, rsp, rt, gn, st, so, g2, w2, gb, rxg, sx, rzh, hb, w3, w3x,
+    eb, fr, fb, zr, stf, acc, ss,
 ):
     dp, hd = lax.axis_index("dp"), lax.axis_index("hd")
     x, zh = lax.rem(hd, NX), lax.div(hd, NX)
@@ -72,13 +72,16 @@
 
     barrier = pltpu.get_barrier_semaphore()
     peer = at(c_=o)
-    partners = [peer]
-    for d in range(1, 16):
+    barrier = pltpu.get_barrier_semaphore()
+    partners = []
+    for d in (8, 7, 9, 6, 10, 5, 11, 4, 12, 3, 13, 2, 14, 1, 15):
         z16 = plus(zh * NZ + z, d, 16)
         partners.append(at(zh_=lax.div(z16, NZ), z_=lax.rem(z16, NZ)))
-    for d in range(1, 16):
+    for d in range(15, 0, -1):
         partners.append(at(x_=plus(x, d % 4, NX), y_=plus(y, d // 4, NY)))
-    for dev in partners:
+    partners.append(peer)
+    partners += [at(x_=plus(x, d, NX), c_=o) for d in (1, 2, 3)]
+    for dev in partners[:15]:
         pl.semaphore_signal(barrier, inc=1, device_id=dev, device_id_type=MESH)
 
     loads = {}
@@ -89,6 +92,8 @@
     for i, (src, dst) in enumerate(pairs):
         loads[i] = pltpu.make_async_copy(src, dst, ls.at[i])
         loads[i].start()
+    for dev in partners[15:]:
+        pl.semaphore_signal(barrier, inc=1, device_id=dev, device_id_type=MESH)
 
     loads[9].wait()
     row = lax.broadcasted_iota(jnp.int32, (64, POS), 0)
@@ -110,7 +115,7 @@
             lat[k, pl.ds(i * 16, 16), :] = la[:, k * 128 : (k + 1) * 128]
     loads[2].wait()
     loads[10].wait()
-    count = counts[0]
+    count = counts[0, 0]
     row8 = lax.broadcasted_iota(jnp.int32, (8, 128), 0)
     live = jnp.where(lax.div(row8, QTOK) < count, F32(1), F32(0))
     for h in range(HEADS):
@@ -132,50 +137,48 @@
 
     w1[...] = jnp.zeros_like(w1)
     loads[5].wait()
-    w1[:OUTCOL, :] = out_proj[...]
+    w1[:OUTCOL, :] = out_proj[:, :512]
+    w1[128 : 128 + OUTCOL, :] = out_proj[:, 512:]
 
     pl.semaphore_wait(barrier, len(partners))
 
-    heads_in, res_in = sems(1), sems(1)
-    go(hsc.at[o], tf.at[c], sending(hsc.at[0]), heads_in, peer)
-    go(rsp.at[o], rt.at[c], sending(rsp.at[0]), res_in, peer)
-    tf[c] = hsc[c]
-    rt[c] = rsp[c]
-    arrive(tf.at[c], heads_in)
-    g1[c, y, z] = tf[...].reshape(16, 512).astype(BF16)
+    g1[c, y, z] = hsc[...].reshape(16, 512).astype(BF16)
 
     def gather_z(g):
-        send, recv = sending(g.at[0, 0, pl.ds(0, 7)]), sems(2)
+        send, recv = sending(g.at[0, 0, pl.ds(0, 7)]), sems(3)
         for j in (7, 6, 5, 4, 3, 2, 1):
-            go(g.at[c, y, z], g.at[c, y, z], send, recv + j // 4, at(z_=flip(z, j)))
+            go(g.at[c, y, z], g.at[c, y, z], send, recv + max(j // 2 - 1, 0), at(z_=flip(z, j)))
         return recv
 
-    def gather_y(g, zrecv, consume):
-        ysend, csend, yrecv, crecv = sending(g.at[0, pl.ds(0, 3)]), sending(g.at[0]), sems(8), sems(4)
-        near = lax.div(z, 4) * 4
-        base = (near, 4 - near)
-        for gi in range(2):
-            arrive(g.at[c, y, pl.ds(base[gi], 3 + gi)], zrecv + gi)
-            part = g.at[c, y, pl.ds(base[gi], 4)]
+    def gather_y(g, zrecv, consume, finish):
+        ysend, csend, yrecv, crecv = sending(g.at[0, pl.ds(0, 3)]), sending(g.at[0]), sems(9), sems(4)
+        parts = ((lax.div(z, 4) * 4, 4), (lax.div(flip(z, 4), 2) * 2, 2), (lax.div(flip(z, 6), 2) * 2, 2))
+        for gi, (base, n) in enumerate(parts):
+            arrive(g.at[c, y, pl.ds(base, n if gi else 3)], zrecv + gi)
+            part = g.at[c, y, pl.ds(base, n)]
             for d in (2, 1, 3):
-                go(part, part, ysend, yrecv + gi * 4 + d, at(y_=plus(y, d, NY)))
+                go(part, part, ysend, yrecv + gi * 3 + d - 1, at(y_=plus(y, d, NY)))
             go(part, part, csend, crecv, peer)
 
         def forward(d):
             yd = plus(y, NY - d, NY)
-            for gi in range(2):
-                part = g.at[c, yd, pl.ds(base[gi], 4)]
-                arrive(part, yrecv + gi * 4 + d)
+            for gi, (base, n) in enumerate(parts):
+                part = g.at[c, yd, pl.ds(base, n)]
+                arrive(part, yrecv + gi * 3 + d - 1)
                 go(part, part, csend, crecv + d, peer)
 
         def take(d):
             yd = plus(y, NY - d, NY)
+            first = consume(g[c, yd].reshape(128, 512), c)
             arrive(g.at[o, yd], crecv + d)
-            consume(yd, d)
+            finish(first, consume(g[o, yd].reshape(128, 512), o), yd, d)
 
         return forward, take
 
-    cps = gather_z(g1)
+    zin = gather_z(g1)
+    res_in = sems(1)
+    go(rsp.at[o], rt.at[c], sending(rsp.at[0]), res_in, peer)
+    rt[c] = rsp[c]
 
     w2[...] = jnp.zeros_like(w2)
     loads[6].wait()
@@ -189,17 +192,22 @@
     ones = jnp.where((r_ == 0) & (c_ >= OUTCOL) & (c_ < OUTCOL + 2), F32(1), F32(0)).astype(BF16)
     for k in range(2):
         w2[k, 2 * UNITS : 2 * UNITS + 16, :128] = ones
-    hb[...] = jnp.zeros_like(hb)
+    mine = c * NX + x
+    for d in range(NY):
+        hb[d, mine, :, 256:] = jnp.zeros((32, 128), BF16)
 
     xt = lax.rem(y, 2) * 2 + lax.div(z, 4)
     here = x == xt
     slot = lax.div(y, 2) * 4 + x
     psend, pself, precv = sending(pb.at[pl.ds(0, 3)]), sending(pb.at[0], jnp.logical_not(here)), sems(2)
 
-    def out_projection(yd, d):
-        left, right = g1[0, yd].reshape(128, 512), g1[1, yd].reshape(128, 512)
-        pv = dot_t(left, w1[:, :512]) + dot_t(right, w1[:, 512:])
-        pb[yd] = pv.astype(BF16).reshape(NZ, 16, 128)
+    def project(block, k):
+        both = dot_t(block, w1[...]).reshape(NZ, 16, 256)
+        return both[:, :8, :128] + both[:, 8:, 128:]
+
+    def out_projection(first, second, yd, d):
+        pv = jnp.stack([jnp.where(c == 0, first, second), jnp.where(c == 0, second, first)], axis=1)
+        pb[yd] = pv.reshape(NZ, 16, 128).astype(BF16)
         cp = copy(pb.at[yd], rx.at[slot], psend if d else pself, precv + lax.div(y, 2), at(x_=xt, y_=yd))
         if d:
             cp.start()
@@ -210,7 +218,7 @@
             def _():
                 rx[slot] = pb[yd]
 
-    forward, take = gather_y(g1, cps, out_projection)
+    forward, take = gather_y(g1, zin, project, out_projection)
     take(0)
     forward(1)
     forward(3)
@@ -251,6 +259,8 @@
     loads[8].wait()
     w3[0, :UNITS, :] = down_w[:, :512]
     w3[1, :UNITS, :384] = down_w[:, 512:]
+    w3_in = sems(1)
+    go(w3.at[o], w3x, sending(w3x), w3_in, peer)
     pl.when(holder)(lambda: arrive(rz.at[pl.ds(0, 7)], zrecv))
     pl.when(jnp.logical_not(holder))(lambda: arrive(rz, zrecv))
 
@@ -268,7 +278,7 @@
     lane = lax.broadcasted_iota(jnp.int32, (16, 512), 1)
     scaled = jnp.where(lane == OUTCOL, high, jnp.where(lane == OUTCOL + 1, low, scaled))
     g2[c, y, z] = scaled.astype(BF16)
-    cps = gather_z(g2)
+    zin = gather_z(g2)
     st[...] = state.reshape(2, 8, 512)
     st_in = sems(1)
     go(st.at[o], so.at[c], sending(st.at[0]), st_in, peer)
@@ -276,10 +286,11 @@
 
     gsend, grecv = sending(gb.at[pl.ds(0, 3)]), sems(4)
 
-    def gate_up(yd, d):
-        left, right = g2[0, yd].reshape(128, 512), g2[1, yd].reshape(128, 512)
-        gu = dot_t(left, w2[0]) + dot_t(right, w2[1])
-        gb[d] = gu.astype(BF16).reshape(NX, 32, 640)
+    def gate_up_half(block, k):
+        return dot_t(block, w2[k])
+
+    def gate_up(first, second, yd, d):
+        gb[d] = (first + second).astype(BF16).reshape(NX, 32, 640)
         for e in (1, 3, 2):
             xd = plus(x, e, NX)
             go(gb.at[d, xd], rxg.at[d, e - 1], gsend, grecv + d, at(x_=xd))
@@ -295,7 +306,7 @@
         sx[d] = tot.astype(BF16)
         go(sx.at[d], rzh.at[d], hsend, hrecv + d, other)
 
-    asend, arecv = sending(hb.at[pl.ds(0, 3)]), sems(4)
+    asend, arecv = [sending(hb.at[0, pl.ds(0, 7)]) for _ in range(NY)], sems(4)
 
     def hidden_units(d):
         arrive(rzh.at[d], hrecv + d)
@@ -303,31 +314,25 @@
         inv = lax.rsqrt(gu[:, 2 * UNITS : 2 * UNITS + 1] / D + 1e-06)
         gate, up = gu[:, :UNITS] * inv, gu[:, UNITS : 2 * UNITS] * inv
         hid = gate / (1.0 + jnp.exp(-gate)) * up
-        hb[d, x, :, :UNITS] = hid.astype(BF16)
-        for e in (1, 3, 2):
-            go(hb.at[d, x], hb.at[d, x], asend, arecv + d, at(x_=plus(x, e, NX)))
-
-    dout, din = sending(dsend), sems(4)
-
-    def down_there(d):
-        arrive(hb.at[d, pl.ds(0, 3)], arecv + d)
-        there = jnp.dot(hb[d].reshape(128, 384), w3[o], preferred_element_type=F32)
-        dsend[d] = there.astype(BF16)
-        go(dsend.at[d], drecv.at[d], dout, din + d, peer)
+        hb[d, mine, :, :UNITS] = hid.astype(BF16)
+        for e in (2, 1, 3, 0):
+            for dev in (at(x_=plus(x, e, NX)), at(x_=plus(x, e, NX), c_=o))[e == 0 :]:
+                go(hb.at[d, mine], hb.at[d, mine], asend[d], arecv + d, dev)
 
     fsend, frecv = sending(eb), sems(1)
 
-    def down_here(d):
-        part = jnp.dot(hb[d].reshape(128, 384), w3[c], preferred_element_type=F32)
-        arrive(drecv.at[d], din + d)
-        part = part + drecv[d].astype(F32)
+    def down(d):
+        arrive(hb.at[d, pl.ds(0, 7)], arecv + d)
+        own_, other_ = hb[d, pl.ds(c * NX, NX)].reshape(128, 384), hb[d, pl.ds(o * NX, NX)].reshape(128, 384)
+        part = jnp.dot(own_, w3[c], preferred_element_type=F32)
+        part = part + jnp.dot(other_, w3x[...], preferred_element_type=F32)
         if d == 0:
             acc[...] = part.reshape(NZ, 16, 512)
         else:
             eb[d - 1] = part.astype(BF16).reshape(NZ, 16, 512)
             go(eb.at[d - 1], fr.at[d - 1], fsend, frecv, at(y_=plus(y, NY - d, NY)))
 
-    forward, take = gather_y(g2, cps, gate_up)
+    forward, take = gather_y(g2, zin, gate_up_half, gate_up)
     take(0)
     forward(1)
     forward(3)
@@ -340,17 +345,14 @@
     sum_x(3)
     sum_x(2)
     hidden_units(0)
-    down_there(0)
+    arrive(w3x, w3_in)
     hidden_units(1)
     hidden_units(3)
-    down_here(0)
+    down(0)
     hidden_units(2)
-    down_there(1)
-    down_there(3)
-    down_here(1)
-    down_here(3)
-    down_there(2)
-    down_here(2)
+    down(1)
+    down(3)
+    down(2)
 
     arrive(so.at[c], st_in)
     for b in range(8):
@@ -358,27 +360,32 @@
         stf[:, b * OUTCOL : (b + 1) * OUTCOL] = so[b % 2, :, lo : lo + OUTCOL]
 
     arrive(fr, frecv)
-    oout, oin = sending(fb.at[pl.ds(0, 7)]), sems(1)
+    oout, oin = sending(fb.at[pl.ds(0, 15)]), sems(1)
 
     def sum_y(t):
         return acc[t] + fr[0, t].astype(F32) + fr[1, t].astype(F32) + fr[2, t].astype(F32)
 
-    for j in (7, 6, 5, 4, 3, 2, 1):
+    for j in (7, 6, 5, 4, 3, 2, 1, 0):
         t = flip(z, j)
-        fb[t] = sum_y(t).astype(BF16)
-        go(fb.at[t], zr.at[j - 1], oout, oin, at(z_=t))
-    tot = sum_y(z)
-    arrive(zr, oin)
-    for j in range(7):
-        tot = tot + zr[j].astype(F32)
-    osum[...] = tot.reshape(2, 8, 512)
-    last = sems(1)
-    go(osum.at[o], orx.at[c], sending(osum.at[0]), last, peer)
-    orx[c] = osum[c]
-    arrive(orx.at[c], last)
+        tot = sum_y(t).astype(BF16).astype(F32)
+        for k in range(2):
+            rows = tot[8 * k : 8 * k + 8]
+            fb[2 * j + k] = jnp.concatenate([rows[:, :256], rows[:, 256:]], axis=0).astype(BF16)
+        if j:
+            for k in range(2):
+                go(fb.at[2 * j + k], zr.at[2 * j + c], oout, oin, at(z_=t, c_=k))
+    go(fb.at[o], zr.at[c], oout, oin, peer)
+    zr[c] = fb[c]
+    arrive(zr.at[pl.ds(0, 15)], oin)
+    cols = []
+    for k in range(2):
+        tot = zr[k].astype(F32)
+        for j in range(1, 8):
+            tot = tot + zr[2 * j + k].astype(F32)
+        cols.append(jnp.concatenate([tot[:8], tot[8:]], axis=1))
     livew = live[:, :1]
-    out[:, :512] = ((stf[:, :512] + orx[0]) * livew).astype(BF16)
-    out[:, 512:] = ((stf[:, 512:] + orx[1, :, :384]) * livew).astype(BF16)
+    out[:, :512] = ((stf[:, :512] + cols[0]) * livew).astype(BF16)
+    out[:, 512:] = ((stf[:, 512:] + cols[1][:, :384]) * livew).astype(BF16)
 
     for when, ref, send in ends:
         if when is None:
@@ -398,15 +405,15 @@
         in_specs=[hbm] * 11,
         out_specs=vmem,
         scratch_shapes=[
-            b(SLOTS, 16, QK), b(SLOTS, POS, QK), pltpu.SMEM((4,), jnp.int32), pltpu.SMEM((1,), jnp.int32), b(HEADS, LAT, 128), b(OUTCOL, 1024), b(8, FEAT), f(7, 128),
+            b(SLOTS, 16, QK), b(SLOTS, POS, QK), pltpu.SMEM((4,), jnp.int32), pltpu.SMEM((1, 1), jnp.int32), b(HEADS, LAT, 128), b(OUTCOL, 1024), b(8, FEAT), f(7, 128),
             b(UNITS, FEAT), b(UNITS, FEAT), b(UNITS, FEAT), pltpu.SemaphoreType.DMA((11,)),
-            f(4, 64, 128), f(2, 8, 512), f(2, 8, 512), b(2, NY, NZ, 16, 512), b(128, 1024),
+            f(4, 64, 128), f(2, 8, 512), b(2, NY, NZ, 16, 512), b(256, 512),
             b(NY, NZ, 16, 128), b(8, NZ, 16, 128), b(16, 16, 128), b(8, 16, 128),
             f(2, 8, 512), f(2, 8, 512), f(2, 1, 512), f(2, 8, 512), f(2, 8, 512),
             b(2, NY, NZ, 16, 512), b(2, 640, 512), b(NY, NX, 32, 640), b(NY, 3, 32, 640),
-            b(NY, 32, 640), b(NY, 32, 640), b(NY, NX, 32, 384), b(2, 384, 512),
-            b(NY, 128, 512), b(NY, 128, 512), b(3, NZ, 16, 512), b(3, NZ, 16, 512),
-            b(NZ, 16, 512), b(7, 16, 512), f(2, 8, 512), f(2, 8, 512), f(8, FEAT), f(NZ, 16, 512),
+            b(NY, 32, 640), b(NY, 32, 640), b(NY, 2 * NX, 32, 384), b(2, 384, 512), b(384, 512),
+            b(3, NZ, 16, 512), b(3, NZ, 16, 512),
+            b(16, 16, 256), b(16, 16, 256), f(8, FEAT), f(NZ, 16, 512),
             pltpu.SemaphoreType.DMA((NSEM,)),
         ],
         compiler_params=pltpu.CompilerParams(
@@ -414,7 +421,7 @@
         ),
         name="decode_layer",
     )(
-        query.reshape(SLOTS, QTOK * HEADS, QK), cache, lengths, counts, value_up, out_proj.T, residual,
+        query.reshape(SLOTS, QTOK * HEADS, QK), cache, lengths, counts.reshape(1, 1), value_up, out_proj.T, residual,
         norm_gain.reshape(7, 128), gate_w.T, up_w.T, down_w,
     )
 

time: 109 us -> 106 us (0.972)
  Pallas kernels: 107 us -> 104 us
    pallas_call x1, Pallas kernels: 107 us -> 104 us  [per_device(): pl.pallas_call(kernel, out_shape=jax.ShapeDtypeStruct((8, FEAT), BF16), i...]
where the time goes in v3:
time: 106 us
  Pallas kernels  104 us (98%)
  local copies, waits for them, and re-layouts  1.31 us (1%)
    pallas_call x1, Pallas kernels, per_device(): pl.pallas_call(kernel, out_shape=jax.ShapeDtypeStruct((8, FEAT), BF16), i...  104 us

profile of v3, /device:TPU:1, one launch (start us, length us, event | category | flops | bytes accessed | tf_op | source)
XLA Modules:
  0.0 105.8 jit_solution(16834336713351646917)
XLA Ops:
  0.7 103.8 %decode_layer.1 = bf16[8,896]{1,0:T(8,128)(2,1)} custom-call(bf16[4,16,576]{2,1,0:T(8,128)(2,1)} %bitcast.10, bf16[4,192,576]{2,1,0:T(8,128)(2,1)} %cache_h.1, s32[4]{0:T(128)} %lengths_h.1, s32[1,1]{1,0:T(1,128)} %bitcast.6.counts_h, bf16[8,512,128]{2,1,0:T(8,128)(2,1)} %value_h.1, bf16[112,1024]{1,0:T(8,128)(2,1)} %bitcast.9, bf16[8,896]{1,0:T(8,128)(2,1)} %res_h.1, ...), custom_call_target="tpu_custom_call" | custom-call | tf_op jit(solution)/shard_map/decode_layer/pallas_call | solution.py:402
  104.4 1.3 %copy.14 = bf16[8,896]{1,0:T(8,128)(2,1)} copy(bf16[8,896]{1,0:T(8,128)(2,1)} %decode_layer.1) | data formatting | bytes 28672

commit v4 on v3

--- a/solution.py
+++ b/solution.py
@@ -21,6 +21,11 @@
         bit = lax.rem(lax.div(value, 1 << i), 2)
         out = out + (1 - bit if (mask >> i) & 1 else bit) * (1 << i)
     return out
+
+
+def apart(a, b, unit):
+    p, q = lax.rem(lax.div(a, unit), 2), lax.rem(lax.div(b, unit), 2)
+    return p + q - 2 * p * q
 
 
 def dot_t(a, b):
@@ -146,8 +151,10 @@
 
     def gather_z(g):
         send, recv = sending(g.at[0, 0, pl.ds(0, 7)]), sems(3)
-        for j in (7, 6, 5, 4, 3, 2, 1):
-            go(g.at[c, y, z], g.at[c, y, z], send, recv + max(j // 2 - 1, 0), at(z_=flip(z, j)))
+        for i in range(6, -1, -1):
+            t = i + jnp.where(z <= i, 1, 0)
+            high, low = apart(z, t, 4), apart(z, t, 2)
+            go(g.at[c, y, z], g.at[c, y, z], send, recv + high * (1 + low), at(z_=t))
         return recv
 
     def gather_y(g, zrecv, consume, finish):
@@ -233,7 +240,7 @@
     z16 = zh * NZ + z
     myslot = zh * 4 + lax.rem(z, 4)
 
-    for k in (1 - zh, zh):
+    for k in (1, 0):
 
         @pl.when(holder)
         def _():
@@ -243,13 +250,9 @@
             tot = rx[4 * k].astype(F32) + rx[4 * k + 1].astype(F32)
             tot = tot + rx[4 * k + 2].astype(F32) + rx[4 * k + 3].astype(F32)
             sb[pl.ds(8 * k, 8)] = tot.astype(BF16)
-            for d in (4, 3, 5, 2, 6, 1, 7, 0):
-                zd = plus(z, d, NZ)
+            for zd in (0, 7, 1, 6, 2, 5, 3, 4):
                 cp = copy(sb.at[8 * k + zd], rz.at[myslot], zsend, zrecv, at(zh_=k, z_=zd))
-                if d:
-                    cp.start()
-                else:
-                    pl.when(k != zh)(cp.start)
+                pl.when(z16 != 8 * k + zd)(cp.start)
 
     @pl.when(holder)
     def _():
@@ -365,17 +368,21 @@
     def sum_y(t):
         return acc[t] + fr[0, t].astype(F32) + fr[1, t].astype(F32) + fr[2, t].astype(F32)
 
-    for j in (7, 6, 5, 4, 3, 2, 1, 0):
-        t = flip(z, j)
+    def last_sum(t):
         tot = sum_y(t).astype(BF16).astype(F32)
         for k in range(2):
             rows = tot[8 * k : 8 * k + 8]
-            fb[2 * j + k] = jnp.concatenate([rows[:, :256], rows[:, 256:]], axis=0).astype(BF16)
-        if j:
-            for k in range(2):
-                go(fb.at[2 * j + k], zr.at[2 * j + c], oout, oin, at(z_=t, c_=k))
-    go(fb.at[o], zr.at[c], oout, oin, peer)
-    zr[c] = fb[c]
+            fb[2 * t + k] = jnp.concatenate([rows[:, :256], rows[:, 256:]], axis=0).astype(BF16)
+
+    me = 2 * z + c
+    for i in range(7):
+        t = i + jnp.where(z <= i, 1, 0)
+        last_sum(t)
+        for k in range(2):
+            go(fb.at[2 * t + k], zr.at[me], oout, oin, at(z_=t, c_=k))
+    last_sum(z)
+    go(fb.at[2 * z + o], zr.at[me], oout, oin, peer)
+    zr[me] = fb[me]
     arrive(zr.at[pl.ds(0, 15)], oin)
     cols = []
     for k in range(2):

time: 106 us -> 104 us (0.981)
  Pallas kernels: 104 us -> 101 us
    pallas_call x1, Pallas kernels: 104 us -> 101 us  [per_device(): pl.pallas_call(kernel, out_shape=jax.ShapeDtypeStruct((8, FEAT), BF16), i...]
where the time goes in v4:
time: 104 us; the launch traced here: 103 us
  Pallas kernels  101 us (97%)
  local copies, waits for them, and re-layouts  1.31 us (1%)
    pallas_call x1, Pallas kernels, per_device(): pl.pallas_call(kernel, out_shape=jax.ShapeDtypeStruct((8, FEAT), BF16), i...  101 us

profile of v4, /device:TPU:1, one launch (start us, length us, event | category | flops | bytes accessed | tf_op | source)
XLA Modules:
  0.0 103.4 jit_solution(16064354566406212862)
XLA Ops:
  0.7 101.5 %decode_layer.1 = bf16[8,896]{1,0:T(8,128)(2,1)} custom-call(bf16[4,16,576]{2,1,0:T(8,128)(2,1)} %bitcast.10, bf16[4,192,576]{2,1,0:T(8,128)(2,1)} %cache_h.1, s32[4]{0:T(128)} %lengths_h.1, s32[1,1]{1,0:T(1,128)} %bitcast.6.counts_h, bf16[8,512,128]{2,1,0:T(8,128)(2,1)} %value_h.1, bf16[112,1024]{1,0:T(8,128)(2,1)} %bitcast.9, bf16[8,896]{1,0:T(8,128)(2,1)} %res_h.1, ...), custom_call_target="tpu_custom_call" | custom-call | tf_op jit(solution)/shard_map/decode_layer/pallas_call | solution.py:409
  102.1 1.3 %copy.14 = bf16[8,896]{1,0:T(8,128)(2,1)} copy(bf16[8,896]{1,0:T(8,128)(2,1)} %decode_layer.1) | data formatting | bytes 28672

commit v5 on v4

--- a/solution.py
+++ b/solution.py
@@ -163,7 +163,7 @@
         for gi, (base, n) in enumerate(parts):
             arrive(g.at[c, y, pl.ds(base, n if gi else 3)], zrecv + gi)
             part = g.at[c, y, pl.ds(base, n)]
-            for d in (2, 1, 3):
+            for d in (1, 3, 2):
                 go(part, part, ysend, yrecv + gi * 3 + d - 1, at(y_=plus(y, d, NY)))
             go(part, part, csend, crecv, peer)
 
@@ -229,8 +229,8 @@
     take(0)
     forward(1)
     forward(3)
+    forward(2)
     take(1)
-    forward(2)
     take(3)
     take(2)
 
@@ -339,23 +339,23 @@
     take(0)
     forward(1)
     forward(3)
+    forward(2)
     take(1)
     sum_x(0)
-    forward(2)
     take(3)
     take(2)
     sum_x(1)
     sum_x(3)
     sum_x(2)
+    arrive(w3x, w3_in)
     hidden_units(0)
-    arrive(w3x, w3_in)
     hidden_units(1)
     hidden_units(3)
-    down(0)
     hidden_units(2)
     down(1)
     down(3)
     down(2)
+    down(0)
 
     arrive(so.at[c], st_in)
     for b in range(8):

time: 104 us -> 103 us (level)
  no operation moved by 1% of the time
where the time goes in v5:
time: 103 us
  Pallas kernels  101 us (98%)
  local copies, waits for them, and re-layouts  1.31 us (1%)
    pallas_call x1, Pallas kernels, per_device(): pl.pallas_call(kernel, out_shape=jax.ShapeDtypeStruct((8, FEAT), BF16), i...  101 us

profile of v5, /device:TPU:1, one launch (start us, length us, event | category | flops | bytes accessed | tf_op | source)
XLA Modules:
  0.0 102.6 jit_solution(14684580161634853393)
XLA Ops:
  0.7 100.6 %decode_layer.1 = bf16[8,896]{1,0:T(8,128)(2,1)} custom-call(bf16[4,16,576]{2,1,0:T(8,128)(2,1)} %bitcast.10, bf16[4,192,576]{2,1,0:T(8,128)(2,1)} %cache_h.1, s32[4]{0:T(128)} %lengths_h.1, s32[1,1]{1,0:T(1,128)} %bitcast.6.counts_h, bf16[8,512,128]{2,1,0:T(8,128)(2,1)} %value_h.1, bf16[112,1024]{1,0:T(8,128)(2,1)} %bitcast.9, bf16[8,896]{1,0:T(8,128)(2,1)} %res_h.1, ...), custom_call_target="tpu_custom_call" | custom-call | tf_op jit(solution)/shard_map/decode_layer/pallas_call | solution.py:409
  101.3 1.3 %copy.14 = bf16[8,896]{1,0:T(8,128)(2,1)} copy(bf16[8,896]{1,0:T(8,128)(2,1)} %decode_layer.1) | data formatting | bytes 28672

commit v6 on v5

--- a/solution.py
+++ b/solution.py
@@ -151,7 +151,7 @@
 
     def gather_z(g):
         send, recv = sending(g.at[0, 0, pl.ds(0, 7)]), sems(3)
-        for i in range(6, -1, -1):
+        for i in (6, 0, 5, 4, 3, 2, 1):
             t = i + jnp.where(z <= i, 1, 0)
             high, low = apart(z, t, 4), apart(z, t, 2)
             go(g.at[c, y, z], g.at[c, y, z], send, recv + high * (1 + low), at(z_=t))
@@ -250,7 +250,7 @@
             tot = rx[4 * k].astype(F32) + rx[4 * k + 1].astype(F32)
             tot = tot + rx[4 * k + 2].astype(F32) + rx[4 * k + 3].astype(F32)
             sb[pl.ds(8 * k, 8)] = tot.astype(BF16)
-            for zd in (0, 7, 1, 6, 2, 5, 3, 4):
+            for zd in (7, 0, 6, 1, 5, 2, 4, 3):
                 cp = copy(sb.at[8 * k + zd], rz.at[myslot], zsend, zrecv, at(zh_=k, z_=zd))
                 pl.when(z16 != 8 * k + zd)(cp.start)
 

time: 103 us -> 102 us (level)
  Pallas kernels: 101 us -> 99.9 us
where the time goes in v6:
time: 102 us
  Pallas kernels  99.9 us (98%)
  local copies, waits for them, and re-layouts  1.31 us (1%)
    pallas_call x1, Pallas kernels, per_device(): pl.pallas_call(kernel, out_shape=jax.ShapeDtypeStruct((8, FEAT), BF16), i...  99.9 us

profile of v6, /device:TPU:1, one launch (start us, length us, event | category | flops | bytes accessed | tf_op | source)
XLA Modules:
  0.0 101.9 jit_solution(9505017605951432034)
XLA Ops:
  0.7 99.9 %decode_layer.1 = bf16[8,896]{1,0:T(8,128)(2,1)} custom-call(bf16[4,16,576]{2,1,0:T(8,128)(2,1)} %bitcast.10, bf16[4,192,576]{2,1,0:T(8,128)(2,1)} %cache_h.1, s32[4]{0:T(128)} %lengths_h.1, s32[1,1]{1,0:T(1,128)} %bitcast.6.counts_h, bf16[8,512,128]{2,1,0:T(8,128)(2,1)} %value_h.1, bf16[112,1024]{1,0:T(8,128)(2,1)} %bitcast.9, bf16[8,896]{1,0:T(8,128)(2,1)} %res_h.1, ...), custom_call_target="tpu_custom_call" | custom-call | tf_op jit(solution)/shard_map/decode_layer/pallas_call | solution.py:409
  100.6 1.3 %copy.14 = bf16[8,896]{1,0:T(8,128)(2,1)} copy(bf16[8,896]{1,0:T(8,128)(2,1)} %decode_layer.1) | data formatting | bytes 28672
